TPU v7x, 128 devices: a whole 4x4x4 slice. The times are simulated.
128 devices in a mesh: row: 8 (over x_lo, y), col: 16 (over x_hi, z, core).
Axes of the slice: x: 4 (x_hi: 2, x_lo: 2; x = x_hi * 2 + x_lo), y: 4, z: 4, core: 2. Of those that a mesh axis runs over, the one named last changes fastest.
Arguments:
- rhs: bfloat16 [1024, 2, 4096], P('col', None, 'row'), may hold values from -6 to 6
- solved: bfloat16 [1024, 49152], P(None, 'col'), may hold values from -6 to 6
- panel: bfloat16 [2, 4096, 49152], P(None, 'row', 'col'), may hold values from -0.02734375 to 0.02734375
- inverse: bfloat16 [2, 4096, 4096], P(None, 'row'), as said below
- link: bfloat16 [4096, 4096], P('row'), may hold values from -0.09375 to 0.09375
Outputs:
- solution: bfloat16 [1024, 2, 4096], P('col', None, 'row')
Inputs may be any that keep to these rules, and one draw needn't show every extreme that they name: Each inverse[b] is upper triangular with diagonal entries between 0.6 and 1.4.
All inputs are finite; a program needn't handle non-finite values.
Results may differ from a plain program's by a relative error of at most 0.0056.
Values may be sent and summed in bfloat16 or wider, within the bound.
A program may use at most 128 MiB of HBM per device.

v0:
```python
import jax
import jax.numpy as jnp
from jax import lax
from jax.sharding import PartitionSpec as P


def contract_rows(left, right):
    return lax.dot_general(
        left, right, (((1,), (1,)), ((), ())), preferred_element_type=jnp.float32
    )


def local(rhs, solved, panel, inverse, link):
    local_rows = panel.shape[1]
    flat_panel = panel.reshape(2 * local_rows, panel.shape[2])
    summed = lax.psum_scatter(
        contract_rows(solved, flat_panel), "col", scatter_dimension=0, tiled=True
    )
    first_sum = summed[:, :local_rows]
    second_sum = summed[:, local_rows:]
    first_res = (rhs[:, 0, :].astype(jnp.float32) - first_sum).astype(jnp.bfloat16)
    first_part = jnp.dot(first_res, inverse[0], preferred_element_type=jnp.float32)
    first_full = lax.psum(first_part, "row").astype(jnp.bfloat16)
    first_own = lax.dynamic_slice_in_dim(
        first_full, lax.axis_index("row") * local_rows, local_rows, 1
    )
    carried = contract_rows(first_full, link)
    second_res = (rhs[:, 1, :].astype(jnp.float32) - second_sum - carried).astype(jnp.bfloat16)
    second_part = jnp.dot(second_res, inverse[1], preferred_element_type=jnp.float32)
    second_own = lax.psum_scatter(second_part, "row", scatter_dimension=1, tiled=True).astype(
        jnp.bfloat16
    )
    return jnp.stack([first_own, second_own], axis=1)


def solution(mesh):
    return jax.shard_map(
        local,
        mesh=mesh,
        in_specs=(
            P("col", None, "row"),
            P(None, "col"),
            P(None, "row", "col"),
            P(None, "row", None),
            P("row", None),
        ),
        out_specs=P("col", None, "row"),
        check_vma=False,
    )
```

profile of v0, /device:TPU:2, one launch (start us, length us, event | category | flops | bytes accessed | tf_op | source)
XLA Modules:
  0.0 222.8 jit_solution(1169902966534646854)
XLA Ops:
  6.5 0.0 reduce-scatter.3.cloned.1.call-start
  6.5 0.0 copy-start
  6.5 12.0 %fusion.11 = f32[1024,1024]{1,0:T(8,128)} fusion(bf16[1024,3072]{1,0:T(8,128)(2,1)} %param.6, bf16[1024,3072]{1,0:T(8,128)(2,1)} %bitcast.27), kind=kOutput, calls=%fused_computation.18 | convolution fusion | flops 6442450944 | bytes 16777216 | tf_op jit(solution)/shard_map/dot_general | solution.py:8
  18.5 0.0 reduce-scatter.3.cloned.1.call-update
  18.6 0.0 reduce-scatter.5.cloned.1.call-start
  18.6 0.0 copy-done
  18.6 0.2 fusion.10
  18.8 82.1 %reduce-scatter.3.cloned.1.call-done = f32[64,1024]{1,0:T(8,128)} async-done(((f32[1024,1024]{1,0:T(8,128)}), f32[64,1024]{1,0:T(8,128)}) %reduce-scatter.3.cloned.1.call-update) | async-done | bytes 262160 | tf_op jit(solution)/shard_map/reduce_scatter | solution.py:16
  100.9 0.0 copy-start.1
  100.9 3.1 %fusion.2 = f32[64,4096]{1,0:T(8,128)S(1)} fusion(bf16[2,512,4096]{2,1,0:T(8,128)(2,1)} %param.8, f32[64,1024]{1,0:T(8,128)} %reduce-scatter.3.cloned.1.call-done, bf16[64,1,512]{2,1,0:T(2,128)(2,1)S(1)} %get-tuple-element.6), kind=kOutput, calls=%fused_computation.2 | convolution fusion | flops 268533760 | bytes 5439488 | tf_op jit(solution)/shard_map/dot_general | solution.py:22
  104.0 67.7 %all-reduce.1 = bf16[64,4096]{1,0:T(8,128)(2,1)S(1)} all-reduce(f32[64,4096]{1,0:T(8,128)S(1)} %fusion.2), channel_id=1, replica_groups=mesh['row'=8,'col'=16] {'row'}, use_global_device_ids=true, to_apply=%region_1.0 | all-reduce | flops 262144 | bytes 1572864 | tf_op jit(solution)/shard_map/psum | solution.py:23
  171.7 0.0 copy-done.1
  171.7 6.7 %fusion = f32[64,4096]{1,0:T(8,128)} fusion(bf16[2,512,4096]{2,1,0:T(8,128)(2,1)} %param.8, bf16[64,4096]{1,0:T(8,128)(2,1)S(1)} %all-reduce.1, bf16[512,4096]{1,0:T(8,128)(2,1)} %param.9, f32[64,1024]{1,0:T(8,128)S(1)} %copy-done.1, bf16[64,1,512]{2,1,0:T(2,128)(2,1)S(1)} %get-tuple-element.5), kind=kOutput, calls=%fused_computation | convolution fusion | flops 537001984 | bytes 10223616 | tf_op jit(solution)/shard_map/dot_general | solution.py:29
  178.4 0.0 reduce-scatter.5.cloned.1.call-update
  178.4 35.8 %reduce-scatter.5.cloned.1.call-done = f32[64,512]{1,0:T(8,128)} async-done(((f32[64,4096]{1,0:T(8,128)}), f32[64,512]{1,0:T(8,128)}) %reduce-scatter.5.cloned.1.call-update) | async-done | bytes 131088 | tf_op jit(solution)/shard_map/reduce_scatter | solution.py:30
  214.2 0.9 convert_bitcast_fusion
  215.1 0.8 copy.8
  (2 shorter events, 0.0 us)
Async XLA Ops:
  6.5 94.3 %reduce-scatter.3.cloned.1.call-start = ((), (), s32[]{:S(2)}) async-start(), calls=%async_computation.2 | async-start | bytes 4456448 | tf_op jit(solution)/shard_map/reduce_scatter | solution.py:16
  6.5 12.1 %copy-start = (bf16[64,2,512]{2,1,0:T(2,128)(2,1)S(1)}, bf16[64,2,512]{2,1,0:T(2,128)(2,1)}, u32[]{:S(2)}) copy-start(bf16[64,2,512]{2,1,0:T(2,128)(2,1)} %param.5) | copy-start | bytes 393220
  18.6 195.6 %reduce-scatter.5.cloned.1.call-start = ((), (), s32[]{:S(2)}) async-start(), calls=%async_computation.3 | async-start | bytes 1179648 | tf_op jit(solution)/shard_map/reduce_scatter | solution.py:30
  100.9 70.8 %copy-start.1 = (f32[64,1024]{1,0:T(8,128)S(1)}, f32[64,1024]{1,0:T(8,128)}, u32[]{:S(2)}) copy-start(f32[64,1024]{1,0:T(8,128)} %reduce-scatter.3.cloned.1.call-done) | copy-start | bytes 786436
Sparse Core Ops, SparseCore 0:
  18.7 82.1 reduce-scatter.2
  178.5 35.6 reduce-scatter.4
where the time goes:
time: 224 us; the launch traced here: 223 us
  waiting for transfers between devices  118 us (53%)
  blocking collectives  67.7 us (30%)
  matrix products  21.8 us (10%)
  between operations  13.5 us (6%)
    reduce_scatter x1, waiting for transfers between devices, local(): lax.psum_scatter(contract_rows(solved, flat_panel), 'col', scatter_dimens...  82.1 us
    psum x1, blocking collectives, local(): first_full = lax.psum(first_part, 'row').astype(jnp.bfloat16)  67.7 us
    reduce_scatter x1, waiting for transfers between devices, local(): lax.psum_scatter(second_part, 'row', scatter_dimension=1, tiled=True)  35.8 us
    dot_general x1, matrix products, contract_rows(): lax.dot_general(left, right, (((1,), (1,)), ((), ())), preferred_element_...  12 us
    dot_general x1, matrix products, local(): jnp.dot(second_res, inverse[1], preferred_element_type=jnp.float32)  6.65 us
  transfers between devices with their start and end apart: 2, of which 2 were waited for; matrix products, arithmetic and copies ran while one was open for 0% of the time, Pallas kernels for 0%

commit v1 on v0

v1 whole, which is shorter than its diff:
```python
import functools

import jax
import jax.numpy as jnp
from jax import lax
from jax.experimental import pallas as pl
from jax.experimental.pallas import tpu as pltpu
from jax.sharding import PartitionSpec as P

MESH = pl.DeviceIdType.MESH
BF16 = jnp.bfloat16
F32 = jnp.float32
NT = (((1,), (1,)), ((), ()))
NN = (((1,), (0,)), ((), ()))
ROWS = 8
Z_OFFSETS = (2, 1, 3, 0)


def dot(left, right, dims):
    return lax.dot_general(left, right, dims, preferred_element_type=F32)


def kernel(
    solved, panel, inverse, link, rhs, out,
    sol_v, pan_v, inv_v, lnk_v, rhs_v,
    core_out, core_in, own, col_out, col_in, res1,
    a_out, a_in, f_all, c_out, c_in,
    load_sem, core_sem, col_sem, a_sem, f_sem, c_sem,
):
    samples, local_rows = rhs.shape[1], rhs.shape[2]
    row, col = lax.axis_index("row"), lax.axis_index("col")
    x_hi, z, core = col // 8, (col // 2) % 4, col % 2

    def col_of(dx, dz, k):
        return lax.rem(x_hi + dx, 2) * 8 + lax.rem(z + dz, 4) * 2 + k

    def rows(slot, count=1):
        return pl.ds(slot * samples, count * samples)

    def remote(src, dst, sems, slot, device):
        return pltpu.make_async_remote_copy(
            src_ref=src, dst_ref=dst, send_sem=sems.at[0, slot], recv_sem=sems.at[1, slot],
            device_id=device, device_id_type=MESH,
        )

    def load_sol(kind, half, j):
        c = col_of(1 - half, Z_OFFSETS[j], 1 - core if kind == 0 else core)
        slot = kind * 8 + half * 4 + j
        return pltpu.make_async_copy(
            solved.at[pl.ds(pl.multiple_of(c * samples, samples), samples)],
            sol_v.at[rows(slot)], load_sem.at[slot],
        )

    load_panel = [pltpu.make_async_copy(panel.at[b], pan_v.at[b], load_sem.at[16 + b]) for b in range(2)]
    load_inv = [pltpu.make_async_copy(inverse.at[b], inv_v.at[b], load_sem.at[18 + b]) for b in range(2)]
    load_link = pltpu.make_async_copy(link, lnk_v, load_sem.at[20])
    load_rhs = pltpu.make_async_copy(rhs, rhs_v, load_sem.at[21])
    load_panel[0].start()
    for half in range(2):
        for kind in range(2):
            for j in range(4):
                load_sol(kind, half, j).start()
    load_panel[1].start()
    load_rhs.start()
    load_inv[0].start()
    load_link.start()
    load_inv[1].start()

    barrier = pltpu.get_barrier_semaphore()
    for i in range(1, ROWS):
        pl.semaphore_signal(barrier, inc=1, device_id=(lax.rem(row + i, ROWS), col), device_id_type=MESH)
    for dx in range(2):
        for dz in range(4):
            if dx or dz:
                pl.semaphore_signal(barrier, inc=1, device_id=(row, col_of(dx, dz, core)), device_id_type=MESH)
    sibling = (row, col_of(0, 0, 1 - core))
    pl.semaphore_signal(barrier, inc=1, device_id=sibling, device_id_type=MESH)
    pl.semaphore_wait(barrier, 15)

    def core_copy(b, half):
        at = rows(half * 4, 4)
        return remote(core_out.at[b, at], core_in.at[b, at], core_sem, b * 2 + half, sibling)

    def col_copy(b, half, j):
        at = rows(half * 4 + j)
        return remote(
            col_out.at[b, at], col_in.at[b, at], col_sem, b * 8 + half * 4 + j,
            (row, col_of(1 - half, Z_OFFSETS[j], core)),
        )

    for b in range(2):
        load_panel[b].wait()
        for half in range(2):
            at = rows(half * 4, 4)
            if b == 0:
                for j in range(4):
                    load_sol(0, half, j).wait()
            core_out[b, at] = dot(sol_v[at], pan_v[b], NT).astype(BF16)
            core_copy(b, half).start()
            if b == 0:
                for j in range(4):
                    load_sol(1, half, j).wait()
            own[...] = dot(sol_v[rows(8 + half * 4, 4)], pan_v[b], NT)
            core_copy(b, half).wait_recv()
            total = own[...] + core_in[b, at].astype(F32)
            if half == 0:
                col_out[b, at] = total.astype(BF16)
            else:
                col_out[b, rows(4, 3)] = total[: 3 * samples].astype(BF16)
                res1[b] = total[3 * samples :]
            for j in range(4):
                if half == 0 or j < 3:
                    col_copy(b, half, j).start()

    def summed(b):
        total = res1[b]
        for half in range(2):
            for j in range(4):
                if half == 0 or j < 3:
                    col_copy(b, half, j).wait_recv()
                    total = total + col_in[b, rows(half * 4 + j)].astype(F32)
        return total

    def cols(index):
        return pl.ds(pl.multiple_of(index * local_rows, local_rows), local_rows)

    def solve(b, res, outgoing, incoming, sems, wait_between=None):
        def copy(i):
            return remote(outgoing.at[i], incoming.at[i], sems, i, (row + i, col))

        for i in reversed(range(1, ROWS)):
            @pl.when(row + i < ROWS)
            def _():
                outgoing[i] = dot(res, inv_v[b, :, cols(row + i)], NN).astype(BF16)
                copy(i).start()

        res1[b] = dot(res, inv_v[b, :, cols(row)], NN)
        for i in range(1, ROWS):
            @pl.when(row >= i)
            def _():
                copy(i).wait_recv()
                res1[b] += incoming[i].astype(F32)

        for i in range(1, ROWS):
            @pl.when(row + i < ROWS)
            def _():
                copy(i).wait_send()

        return res1[b].astype(BF16)

    load_rhs.wait()
    res0 = (rhs_v[0].astype(F32) - summed(0)).astype(BF16)
    load_inv[0].wait()
    first = solve(0, res0, a_out, a_in, a_sem)
    f_all[0] = first
    out[0] = first

    def f_copy(i):
        return remote(f_all.at[0], f_all.at[i], f_sem, i, (lax.rem(row + i, ROWS), col))

    for i in range(1, ROWS):
        f_copy(i).start()
    rest = rhs_v[1].astype(F32) - summed(1)
    load_link.wait()
    rest = rest - dot(f_all[0], lnk_v[:, cols(row)], NT)
    res1[1] = rest
    for i in range(1, ROWS):
        f_copy(i).wait_recv()
        res1[1] -= dot(f_all[i], lnk_v[:, cols(lax.rem(row + ROWS - i, ROWS))], NT)
    load_inv[1].wait()
    out[1] = solve(1, res1[1].astype(BF16), c_out, c_in, c_sem)

    for i in range(1, ROWS):
        f_copy(i).wait_send()
    for b in range(2):
        for half in range(2):
            core_copy(b, half).wait_send()
            for j in range(4):
                if half == 0 or j < 3:
                    col_copy(b, half, j).wait_send()


def local(rhs, solved, panel, inverse, link):
    samples, _, local_rows = rhs.shape
    depth, total = solved.shape[1], solved.shape[0]
    block = (samples, local_rows)
    any_spec = pl.BlockSpec(memory_space=pl.ANY)
    parts = pl.pallas_call(
        kernel,
        out_shape=jax.ShapeDtypeStruct((2,) + block, BF16),
        in_specs=[any_spec] * 5,
        out_specs=pl.BlockSpec(memory_space=pltpu.VMEM),
        scratch_shapes=[
            pltpu.VMEM(solved.shape, BF16),
            pltpu.VMEM(panel.shape, BF16),
            pltpu.VMEM(inverse.shape, BF16),
            pltpu.VMEM(link.shape, BF16),
            pltpu.VMEM((2,) + block, BF16),
            pltpu.VMEM((2, 8 * samples, local_rows), BF16),
            pltpu.VMEM((2, 8 * samples, local_rows), BF16),
            pltpu.VMEM((4 * samples, local_rows), F32),
            pltpu.VMEM((2, 8 * samples, local_rows), BF16),
            pltpu.VMEM((2, 8 * samples, local_rows), BF16),
            pltpu.VMEM((2,) + block, F32),
            pltpu.VMEM((8,) + block, BF16),
            pltpu.VMEM((8,) + block, BF16),
            pltpu.VMEM((8,) + block, BF16),
            pltpu.VMEM((8,) + block, BF16),
            pltpu.VMEM((8,) + block, BF16),
            pltpu.SemaphoreType.DMA((22,)),
            pltpu.SemaphoreType.DMA((2, 4)),
            pltpu.SemaphoreType.DMA((2, 16)),
            pltpu.SemaphoreType.DMA((2, 8)),
            pltpu.SemaphoreType.DMA((2, 8)),
            pltpu.SemaphoreType.DMA((2, 8)),
        ],
        compiler_params=pltpu.CompilerParams(
            collective_id=0, has_side_effects=True, vmem_limit_bytes=56 << 20
        ),
        cost_estimate=pl.CostEstimate(
            flops=4 * total * depth * local_rows, bytes_accessed=24 << 20, transcendentals=0
        ),
        name="window_solve",
    )(solved, panel, inverse, link, rhs.transpose(1, 0, 2))
    return parts.transpose(1, 0, 2)


def solution(mesh):
    return jax.shard_map(
        local,
        mesh=mesh,
        in_specs=(
            P("col", None, "row"),
            P(None, "col"),
            P(None, "row", "col"),
            P(None, "row", None),
            P("row", None),
        ),
        out_specs=P("col", None, "row"),
        check_vma=False,
    )
```

time: 224 us -> 52.7 us (0.24)
  waiting for transfers between devices: 118 us -> 0 us
  blocking collectives: 67.7 us -> 0 us
  Pallas kernels: 0 us -> 49.2 us
  matrix products: 21.8 us -> 0 us
  between operations: 13.5 us -> 0.01 us
  local copies, waits for them, and re-layouts: 1 us -> 3.27 us
    reduce_scatter x2 -> x0, waiting for transfers between devices: 118 us -> none  [the longest x1 82.1 us: local(): lax.psum_scatter(contract_rows(solved, flat_panel), 'col', scatter_dimens...]
    psum x1 -> x0, blocking collectives: 67.7 us -> none  [local(): first_full = lax.psum(first_part, 'row').astype(jnp.bfloat16)]
    pallas_call x0 -> x1, Pallas kernels: none -> 49.2 us  [local(): pl.pallas_call(kernel, out_shape=jax.ShapeDtypeStruct((2,) + block, BF16)...]
    dot_general x3 -> x0, matrix products: 21.8 us -> none  [the longest x1 12 us: contract_rows(): lax.dot_general(left, right, (((1,), (1,)), ((), ())), preferred_element_...]
  transfers between devices with their start and end apart: 2 -> 0, of which waited for: 2 -> 0; matrix products, arithmetic and copies ran while one was open for 0% -> 0% of each run, Pallas kernels for 0% -> 0%
where the time goes in v1:
time: 52.7 us; the launch traced here: 52.5 us
  Pallas kernels  49.2 us (93%)
  local copies, waits for them, and re-layouts  3.27 us (6%)
    pallas_call x1, Pallas kernels, local(): pl.pallas_call(kernel, out_shape=jax.ShapeDtypeStruct((2,) + block, BF16)...  49.2 us
    transpose x1, local copies, waits for them, and re-layouts, local(): return parts.transpose(1, 0, 2)  1.7 us
    unnamed x1, local copies, waits for them, and re-layouts  1.57 us

profile of v1, /device:TPU:2, one launch (start us, length us, event | category | flops | bytes accessed | tf_op | source)
XLA Modules:
  0.0 52.5 jit_solution(7175304238727651970)
XLA Ops:
  0.0 1.6 %copy.9 = bf16[64,2,512]{2,0,1:T(8,128)(2,1)} copy(bf16[64,2,512]{2,1,0:T(2,128)(2,1)} %param.5) | data formatting | bytes 262144 | tf_op args[0]
  1.6 49.2 %window_solve.1 = bf16[2,64,512]{2,1,0:T(8,128)(2,1)} custom-call(bf16[1024,3072]{1,0:T(8,128)(2,1)} %solved.1, bf16[2,512,3072]{2,1,0:T(8,128)(2,1)} %panel.1, bf16[2,512,4096]{2,1,0:T(8,128)(2,1)} %inverse.1, bf16[512,4096]{1,0:T(8,128)(2,1)} %link.1, bf16[2,64,512]{2,1,0:T(8,128)(2,1)} %bitcast.5), custom_call_target="tpu_custom_call" | custom-call | flops 6442450944 | bytes 25165824 | tf_op jit(solution)/shard_map/window_solve/pallas_call | solution.py:188
  50.8 1.7 %copy.7 = bf16[64,2,512]{2,1,0:T(2,128)(2,1)} copy(bf16[64,2,512]{2,0,1:T(8,128)(2,1)} %bitcast.4) | data formatting | bytes 262144 | tf_op jit(solution)/shard_map/transpose | solution.py:225

commit v2 on v0

v2 whole, which is shorter than its diff:
```python
import functools

import jax
import jax.numpy as jnp
from jax import lax
from jax.experimental import pallas as pl
from jax.experimental.pallas import tpu as pltpu
from jax.sharding import PartitionSpec as P

MESH = pl.DeviceIdType.MESH
BF16 = jnp.bfloat16
F32 = jnp.float32
NT = (((1,), (1,)), ((), ()))
NN = (((1,), (0,)), ((), ()))
ROWS = 8
SLOTS = 8
Z_OFFSETS = (2, 1, 3, 0)
HALVES = 2


def dot(left, right, dims):
    return lax.dot_general(left, right, dims, preferred_element_type=F32)


def kernel(
    stages, solved, panel, inverse, link, rhs, out,
    sol_v, pan_v, inv_v, lnk_v, rhs_v,
    core_out, core_in, col_out, col_in, x_out, x_in, keep, acc,
    part, a_out, a_in, f_all, c_out, c_in,
    load_sem, core_sem, col_sem, x_sem, a_sem, f_sem, c_sem,
):
    samples, local_rows = rhs.shape[0], rhs.shape[2]
    part_rows = samples // HALVES
    row, col = lax.axis_index("row"), lax.axis_index("col")
    x_lo = row // 4
    x_hi, z, core = col // 8, (col // 2) % 4, col % 2
    drains, arrivals = [], {}

    def col_of(dx, dz, k):
        return lax.rem(x_hi + dx, 2) * 8 + lax.rem(z + dz, 4) * 2 + k

    def remote(src, dst, send_sem, recv_sem, device):
        return pltpu.make_async_remote_copy(
            src_ref=src, dst_ref=dst, send_sem=send_sem, recv_sem=recv_sem,
            device_id=device, device_id_type=MESH,
        )

    def start(copy, *key):
        copy.start()
        drains.append(copy.wait_send)
        arrivals[key] = copy.wait_recv

    def arrive(*key):
        arrivals.pop(key)()

    def slot_of(s):
        return Z_OFFSETS[s // 2], 1 - s % 2

    def slot_rows(s, count=1):
        return pl.ds(s * part_rows, count * part_rows)

    def load_sol(kind, h, s):
        dz, dx = slot_of(s)
        c = col_of(dx, dz, 1 - core if kind == 0 else core)
        at = pl.multiple_of(c * samples + h * part_rows, part_rows)
        return pltpu.make_async_copy(
            solved.at[pl.ds(at, part_rows)], sol_v.at[kind, h, slot_rows(s)],
            load_sem.at[(kind * HALVES + h) * SLOTS + s],
        )

    load_panel = [pltpu.make_async_copy(panel.at[b], pan_v.at[b], load_sem.at[32 + b]) for b in range(2)]
    load_inv = [pltpu.make_async_copy(inverse.at[b], inv_v.at[b], load_sem.at[34 + b]) for b in range(2)]
    load_link = pltpu.make_async_copy(link, lnk_v, load_sem.at[36])
    load_rhs = pltpu.make_async_copy(rhs, rhs_v, load_sem.at[37])
    def load(copy, *key):
        copy.start()
        arrivals[key] = copy.wait

    load(load_rhs, "rhs")
    load(load_panel[0], "panel", 0)
    for h in range(HALVES):
        for kind in range(2):
            for s in range(SLOTS):
                load(load_sol(kind, h, s), "sol", kind, h, s)
    load(load_panel[1], "panel", 1)
    load(load_inv[0], "inverse", 0)
    load(load_link, "link")
    load(load_inv[1], "inverse", 1)

    barrier = pltpu.get_barrier_semaphore()
    for i in range(1, ROWS):
        pl.semaphore_signal(barrier, inc=1, device_id=(lax.rem(row + i, ROWS), col), device_id_type=MESH)
    for s in range(SLOTS - 1):
        dz, dx = slot_of(s)
        pl.semaphore_signal(barrier, inc=1, device_id=(row, col_of(dx, dz, core)), device_id_type=MESH)
    sibling = (row, col_of(0, 0, 1 - core))
    pl.semaphore_signal(barrier, inc=1, device_id=sibling, device_id_type=MESH)

    arrive("rhs")
    rhs_all = rhs_v[...].astype(F32)
    for b in range(2):
        for h in range(HALVES):
            acc[b, h] = rhs_all[h * part_rows : (h + 1) * part_rows, b, :]

    pl.semaphore_wait(barrier, 15)

    def core_copy(b, h):
        return remote(core_out.at[b, h], core_in.at[b, h], core_sem.at[0, b, h], core_sem.at[1, b, h], sibling)

    def col_copy(h, s):
        dz, dx = slot_of(s)
        return remote(
            col_out.at[0, h, slot_rows(s)], col_in.at[0, h, slot_rows(s)],
            col_sem.at[0, 0, h, s], col_sem.at[1, 0, h, s], (row, col_of(dx, dz, core)),
        )

    def z_copy(h, i):
        at = slot_rows(2 * i, 2)
        return remote(
            col_out.at[1, h, at], col_in.at[1, h, at],
            col_sem.at[0, 1, h, i], col_sem.at[1, 1, h, i], (row, col_of(0, Z_OFFSETS[i], core)),
        )

    def x_copy(h):
        return remote(x_out.at[h], x_in.at[h], x_sem.at[0, h], x_sem.at[1, h], (row, col_of(1, 0, core)))

    def sibling_part(b, h):
        if b == 0:
            for s in range(SLOTS):
                arrive("sol", 0, h, s)
        if h == 0:
            arrive("panel", b)
        core_out[b, h] = dot(sol_v[0, h], pan_v[b], NT).astype(BF16)
        start(core_copy(b, h), "core", b, h)

    def own_part(b, h):
        if b == 0:
            for s in range(SLOTS):
                arrive("sol", 1, h, s)
        total = dot(sol_v[1, h], pan_v[b], NT)
        arrive("core", b, h)
        total = total + core_in[b, h].astype(F32)
        last = 7 * part_rows
        if b == 0:
            col_out[0, h, slot_rows(0, 7)] = total[:last].astype(BF16)
            for s in range(SLOTS - 1):
                start(col_copy(h, s), "col", h, s)
        else:
            col_out[1, h, slot_rows(0, 6)] = total[: 6 * part_rows].astype(BF16)
            for i in range(3):
                start(z_copy(h, i), "z", h, i)
            keep[h] = total[6 * part_rows : last]
        acc[b, h] -= total[last:]

    def first_residual(h):
        res = acc[0, h]
        for s in range(SLOTS - 1):
            arrive("col", h, s)
            res = res - col_in[0, h, slot_rows(s)].astype(F32)
        return res.astype(BF16)

    def second_sum_over_z(h):
        there, here = keep[h], acc[1, h]
        for i in range(3):
            arrive("z", h, i)
            there = there + col_in[1, h, slot_rows(2 * i)].astype(F32)
            here = here - col_in[1, h, slot_rows(2 * i + 1)].astype(F32)
        x_out[h] = there.astype(BF16)
        start(x_copy(h), "x", h)
        acc[1, h] = here

    def solve_copy(outgoing, incoming, sems, h, j):
        return remote(outgoing.at[h, j], incoming.at[h, row], sems.at[0, h, j], sems.at[1, h, row], (j, col))

    def solve_send(b, h, res, outgoing, incoming, sems):
        def group(js):
            for j in js:
                product = dot(res, inv_v[b, :, j * local_rows : (j + 1) * local_rows], NN)
                part[b, h, j] = product
                outgoing[h, j] = product.astype(BF16)
            for j in js:
                @pl.when(row < j)
                def _():
                    solve_copy(outgoing, incoming, sems, h, j).start()

        group(range(ROWS - 1, 3, -1))

        @pl.when(row < 4)
        def _():
            group(range(3, -1, -1))

        def drain():
            for j in range(1, ROWS):
                @pl.when(row < j)
                def _():
                    solve_copy(outgoing, incoming, sems, h, j).wait_send()

        def wait(i):
            pltpu.make_async_remote_copy(
                src_ref=incoming.at[h, i], dst_ref=incoming.at[h, i],
                send_sem=sems.at[0, h, i], recv_sem=sems.at[1, h, i],
                device_id=(row, col), device_id_type=MESH,
            ).wait_recv()

        def add(i):
            wait(i)
            part[b, h, row] += incoming[h, i].astype(F32)

        def receive():
            for i in range(ROWS - 2, -1, -1):
                pl.when(row > i)(functools.partial(add, i))

        drains.append(drain)
        arrivals["solve", b, h] = receive

    def solve_receive(b, h):
        arrive("solve", b, h)

        return part[b, h, row].astype(BF16)

    def f_copy(h, i):
        return remote(
            f_all.at[h, row], f_all.at[h, row], f_sem.at[0, h, i], f_sem.at[1, h, i],
            (lax.rem(row + i, ROWS), col),
        )

    def first_send(h):
        f_all[h, row] = solve_receive(0, h)
        for i in (6, 5, 7, 4, 3, 2, 1):
            start(f_copy(h, i), "f", h, i)

    def carry(h):
        arrive("x", h)
        res = acc[1, h] - x_in[h].astype(F32)

        def term(owner):
            at = pl.ds(pl.multiple_of(owner * local_rows, local_rows), local_rows)
            return dot(f_all[h, owner], lnk_v[:, at], NT)

        res = res - term(row)
        for i in (1, 7, 2, 6, 3, 5, 4):
            arrive("f", h, i)
            res = res - term(lax.rem(row + ROWS - i, ROWS))
        solve_send(1, h, res.astype(BF16), c_out, c_in, c_sem)

    def finish(h):
        second = solve_receive(1, h)
        both = jnp.stack([f_all[h, row].astype(F32), second.astype(F32)], axis=1)
        out[pl.ds(h * part_rows, part_rows)] = both.astype(BF16)

    def a_step(h):
        if h == 0:
            arrive("inverse", 0)
        solve_send(0, h, first_residual(h), a_out, a_in, a_sem)

    def carry_step(h):
        if h == 0:
            arrive("link")
            arrive("inverse", 1)
        carry(h)

    program = (
        lambda: sibling_part(0, 0), lambda: own_part(0, 0),
        lambda: sibling_part(0, 1), lambda: own_part(0, 1),
        lambda: sibling_part(1, 0), lambda: own_part(1, 0),
        lambda: sibling_part(1, 1),
        lambda: a_step(0),
        lambda: own_part(1, 1),
        lambda: a_step(1),
        lambda: first_send(0),
        lambda: second_sum_over_z(0), lambda: second_sum_over_z(1),
        lambda: first_send(1),
        lambda: carry_step(0), lambda: carry_step(1),
        lambda: finish(0), lambda: finish(1),
    )
    for step in program[:stages]:
        step()
    for wait in [*arrivals.values(), *drains]:
        wait()


def local(rhs, solved, panel, inverse, link, stages=None):
    samples, _, local_rows = rhs.shape
    part_rows = samples // HALVES
    piece = (part_rows, local_rows)
    column = (HALVES, SLOTS * part_rows, local_rows)
    any_spec = pl.BlockSpec(memory_space=pl.ANY)
    dma = pltpu.SemaphoreType.DMA
    return pl.pallas_call(
        functools.partial(kernel, stages),
        out_shape=jax.ShapeDtypeStruct(rhs.shape, BF16),
        in_specs=[any_spec] * 5,
        out_specs=pl.BlockSpec(memory_space=pltpu.VMEM),
        scratch_shapes=[
            pltpu.VMEM((2, HALVES, SLOTS * part_rows, solved.shape[1]), BF16),
            pltpu.VMEM(panel.shape, BF16),
            pltpu.VMEM(inverse.shape, BF16),
            pltpu.VMEM(link.shape, BF16),
            pltpu.VMEM(rhs.shape, BF16),
            pltpu.VMEM((2,) + column, BF16),
            pltpu.VMEM((2,) + column, BF16),
            pltpu.VMEM((2,) + column, BF16),
            pltpu.VMEM((2,) + column, BF16),
            pltpu.VMEM((HALVES,) + piece, BF16),
            pltpu.VMEM((HALVES,) + piece, BF16),
            pltpu.VMEM((HALVES,) + piece, F32),
            pltpu.VMEM((2, HALVES) + piece, F32),
            pltpu.VMEM((2, HALVES, ROWS) + piece, F32),
            pltpu.VMEM((HALVES, ROWS) + piece, BF16),
            pltpu.VMEM((HALVES, ROWS) + piece, BF16),
            pltpu.VMEM((HALVES, ROWS) + piece, BF16),
            pltpu.VMEM((HALVES, ROWS) + piece, BF16),
            pltpu.VMEM((HALVES, ROWS) + piece, BF16),
            dma((38,)),
            dma((2, 2, HALVES)),
            dma((2, 2, HALVES, SLOTS)),
            dma((2, HALVES)),
            dma((2, HALVES, ROWS)),
            dma((2, HALVES, ROWS)),
            dma((2, HALVES, ROWS)),
        ],
        compiler_params=pltpu.CompilerParams(
            collective_id=0 if stages is None else stages, has_side_effects=True, vmem_limit_bytes=56 << 20
        ),
        cost_estimate=pl.CostEstimate(
            flops=4 * solved.shape[0] * solved.shape[1] * local_rows, bytes_accessed=24 << 20, transcendentals=0
        ),
        name="window_solve" if stages is None else f"stage{stages:02d}",
    )(solved, panel, inverse, link, rhs)


def solution(mesh):
    return jax.shard_map(
        local,
        mesh=mesh,
        in_specs=(
            P("col", None, "row"),
            P(None, "col"),
            P(None, "row", "col"),
            P(None, "row", None),
            P("row", None),
        ),
        out_specs=P("col", None, "row"),
        check_vma=False,
    )
```

time: 224 us -> 46.5 us (0.21)
  waiting for transfers between devices: 118 us -> 0 us
  blocking collectives: 67.7 us -> 0 us
  Pallas kernels: 0 us -> 44.7 us
  matrix products: 21.8 us -> 0 us
  between operations: 13.5 us -> 0.01 us
    reduce_scatter x2 -> x0, waiting for transfers between devices: 118 us -> none  [the longest x1 82.1 us: local(): lax.psum_scatter(contract_rows(solved, flat_panel), 'col', scatter_dimens...]
    psum x1 -> x0, blocking collectives: 67.7 us -> none  [local(): first_full = lax.psum(first_part, 'row').astype(jnp.bfloat16)]
    pallas_call x0 -> x1, Pallas kernels: none -> 44.7 us  [local(): pl.pallas_call(functools.partial(kernel, stages), out_shape=jax.ShapeDtyp...]
    dot_general x3 -> x0, matrix products: 21.8 us -> none  [the longest x1 12 us: contract_rows(): lax.dot_general(left, right, (((1,), (1,)), ((), ())), preferred_element_...]
  transfers between devices with their start and end apart: 2 -> 0, of which waited for: 2 -> 0; matrix products, arithmetic and copies ran while one was open for 0% -> 0% of each run, Pallas kernels for 0% -> 0%
where the time goes in v2:
time: 46.5 us; the launch traced here: 46.4 us
  Pallas kernels  44.7 us (96%)
  local copies, waits for them, and re-layouts  1.65 us (4%)
    pallas_call x1, Pallas kernels, local(): pl.pallas_call(functools.partial(kernel, stages), out_shape=jax.ShapeDtyp...  44.7 us
    unnamed x1, local copies, waits for them, and re-layouts  1.65 us

profile of v2, /device:TPU:2, one launch (start us, length us, event | category | flops | bytes accessed | tf_op | source)
XLA Modules:
  0.0 46.4 jit_solution(8593930594550733444)
XLA Ops:
  0.0 44.7 %window_solve.1 = bf16[64,2,512]{2,1,0:T(2,128)(2,1)} custom-call(bf16[1024,3072]{1,0:T(8,128)(2,1)} %solved.1, bf16[2,512,3072]{2,1,0:T(8,128)(2,1)} %panel.1, bf16[2,512,4096]{2,1,0:T(8,128)(2,1)} %inverse.1, bf16[512,4096]{1,0:T(8,128)(2,1)} %link.1, bf16[64,2,512]{2,1,0:T(2,128)(2,1)} %rhs.1), custom_call_target="tpu_custom_call" | custom-call | flops 6442450944 | bytes 25165824 | tf_op jit(solution)/shard_map/window_solve/pallas_call | solution.py:289
  44.8 1.7 %copy.7 = bf16[64,2,512]{2,1,0:T(2,128)(2,1)} copy(bf16[64,2,512]{2,1,0:T(2,128)(2,1)} %window_solve.1) | data formatting | bytes 262144

commit v3 on v2

--- a/solution.py
+++ b/solution.py
@@ -76,16 +76,16 @@
         copy.start()
         arrivals[key] = copy.wait
 
+    def load_half(kind, h):
+        for s in range(SLOTS):
+            load(load_sol(kind, h, s), "sol", kind, h, s)
+
+    load(load_panel[0], "panel", 0)
+    load_half(0, 0)
+    load_half(1, 0)
     load(load_rhs, "rhs")
-    load(load_panel[0], "panel", 0)
-    for h in range(HALVES):
-        for kind in range(2):
-            for s in range(SLOTS):
-                load(load_sol(kind, h, s), "sol", kind, h, s)
-    load(load_panel[1], "panel", 1)
-    load(load_inv[0], "inverse", 0)
-    load(load_link, "link")
-    load(load_inv[1], "inverse", 1)
+    load_half(0, 1)
+    load_half(1, 1)
 
     barrier = pltpu.get_barrier_semaphore()
     for i in range(1, ROWS):
@@ -96,13 +96,12 @@
     sibling = (row, col_of(0, 0, 1 - core))
     pl.semaphore_signal(barrier, inc=1, device_id=sibling, device_id_type=MESH)
 
-    arrive("rhs")
-    rhs_all = rhs_v[...].astype(F32)
-    for b in range(2):
-        for h in range(HALVES):
-            acc[b, h] = rhs_all[h * part_rows : (h + 1) * part_rows, b, :]
-
-    pl.semaphore_wait(barrier, 15)
+    def take_rhs():
+        arrive("rhs")
+        rhs_all = rhs_v[...].astype(F32)
+        for b in range(2):
+            for h in range(HALVES):
+                acc[b, h] = rhs_all[h * part_rows : (h + 1) * part_rows, b, :]
 
     def core_copy(b, h):
         return remote(core_out.at[b, h], core_in.at[b, h], core_sem.at[0, b, h], core_sem.at[1, b, h], sibling)
@@ -130,14 +129,25 @@
                 arrive("sol", 0, h, s)
         if h == 0:
             arrive("panel", b)
+        if (b, h) == (0, 1):
+            load(load_panel[1], "panel", 1)
+            load(load_inv[0], "inverse", 0)
         core_out[b, h] = dot(sol_v[0, h], pan_v[b], NT).astype(BF16)
+        if (b, h) == (0, 0):
+            pl.semaphore_wait(barrier, 15)
         start(core_copy(b, h), "core", b, h)
 
     def own_part(b, h):
         if b == 0:
             for s in range(SLOTS):
                 arrive("sol", 1, h, s)
+        if (b, h) == (1, 0):
+            load(load_link, "link")
+            load(load_inv[1], "inverse", 1)
         total = dot(sol_v[1, h], pan_v[b], NT)
+        if (b, h) == (0, 0):
+            clear()
+            take_rhs()
         arrive("core", b, h)
         total = total + core_in[b, h].astype(F32)
         last = 7 * part_rows
@@ -153,16 +163,18 @@
         acc[b, h] -= total[last:]
 
     def first_residual(h):
+        for s in range(SLOTS - 1):
+            arrive("col", h, s)
         res = acc[0, h]
         for s in range(SLOTS - 1):
-            arrive("col", h, s)
             res = res - col_in[0, h, slot_rows(s)].astype(F32)
         return res.astype(BF16)
 
     def second_sum_over_z(h):
+        for i in range(3):
+            arrive("z", h, i)
         there, here = keep[h], acc[1, h]
         for i in range(3):
-            arrive("z", h, i)
             there = there + col_in[1, h, slot_rows(2 * i)].astype(F32)
             here = here - col_in[1, h, slot_rows(2 * i + 1)].astype(F32)
         x_out[h] = there.astype(BF16)
@@ -202,34 +214,53 @@
                 device_id=(row, col), device_id_type=MESH,
             ).wait_recv()
 
-        def add(i):
-            wait(i)
-            part[b, h, row] += incoming[h, i].astype(F32)
-
         def receive():
-            for i in range(ROWS - 2, -1, -1):
-                pl.when(row > i)(functools.partial(add, i))
+            for i in range(ROWS - 1):
+                pl.when(row > i)(functools.partial(wait, i))
 
         drains.append(drain)
         arrivals["solve", b, h] = receive
 
-    def solve_receive(b, h):
+    def solve_receive(b, h, incoming):
         arrive("solve", b, h)
-
-        return part[b, h, row].astype(BF16)
+        total = part[b, h, row]
+        for i in range(ROWS - 1):
+            total = total + incoming[h, i].astype(F32)
+        return total.astype(BF16)
+
+    def clear():
+        for i in range(ROWS - 1):
+            @pl.when(row <= i)
+            def _():
+                a_in[:, i] = jnp.zeros_like(a_in[:, i])
+                c_in[:, i] = jnp.zeros_like(c_in[:, i])
 
     def f_copy(h, i):
         return remote(
-            f_all.at[h, row], f_all.at[h, row], f_sem.at[0, h, i], f_sem.at[1, h, i],
+            f_all.at[h, row], f_all.at[h, row], f_sem.at[0, h, i], f_sem.at[1, h, row],
             (lax.rem(row + i, ROWS), col),
         )
 
+    def f_wait(h, owner):
+        remote(
+            f_all.at[h, owner], f_all.at[h, owner], f_sem.at[0, h, owner], f_sem.at[1, h, owner], (row, col)
+        ).wait_recv()
+
     def first_send(h):
-        f_all[h, row] = solve_receive(0, h)
+        f_all[h, row] = solve_receive(0, h, a_in)
         for i in (6, 5, 7, 4, 3, 2, 1):
-            start(f_copy(h, i), "f", h, i)
+            copy = f_copy(h, i)
+            copy.start()
+            drains.append(copy.wait_send)
+
+        def receive():
+            for owner in range(ROWS):
+                pl.when(row != owner)(functools.partial(f_wait, h, owner))
+
+        arrivals["f", h] = receive
 
     def carry(h):
+        arrivals.pop(("f", h))
         arrive("x", h)
         res = acc[1, h] - x_in[h].astype(F32)
 
@@ -237,14 +268,17 @@
             at = pl.ds(pl.multiple_of(owner * local_rows, local_rows), local_rows)
             return dot(f_all[h, owner], lnk_v[:, at], NT)
 
-        res = res - term(row)
-        for i in (1, 7, 2, 6, 3, 5, 4):
-            arrive("f", h, i)
-            res = res - term(lax.rem(row + ROWS - i, ROWS))
+        for other in range(2):
+            base = lax.rem(x_lo + other, 2) * 4
+            for i in range(4):
+                @pl.when(base + i != row)
+                def _():
+                    f_wait(h, base + i)
+            res = res - sum(term(base + i) for i in range(4))
         solve_send(1, h, res.astype(BF16), c_out, c_in, c_sem)
 
     def finish(h):
-        second = solve_receive(1, h)
+        second = solve_receive(1, h, c_in)
         both = jnp.stack([f_all[h, row].astype(F32), second.astype(F32)], axis=1)
         out[pl.ds(h * part_rows, part_rows)] = both.astype(BF16)
 
@@ -263,13 +297,14 @@
         lambda: sibling_part(0, 0), lambda: own_part(0, 0),
         lambda: sibling_part(0, 1), lambda: own_part(0, 1),
         lambda: sibling_part(1, 0), lambda: own_part(1, 0),
+        lambda: a_step(0),
         lambda: sibling_part(1, 1),
-        lambda: a_step(0),
+        lambda: a_step(1),
         lambda: own_part(1, 1),
-        lambda: a_step(1),
         lambda: first_send(0),
-        lambda: second_sum_over_z(0), lambda: second_sum_over_z(1),
+        lambda: second_sum_over_z(0),
         lambda: first_send(1),
+        lambda: second_sum_over_z(1),
         lambda: carry_step(0), lambda: carry_step(1),
         lambda: finish(0), lambda: finish(1),
     )
@@ -288,7 +323,7 @@
     dma = pltpu.SemaphoreType.DMA
     return pl.pallas_call(
         functools.partial(kernel, stages),
-        out_shape=jax.ShapeDtypeStruct(rhs.shape, BF16),
+        out_shape=pltpu.VMEM(rhs.shape, BF16),
         in_specs=[any_spec] * 5,
         out_specs=pl.BlockSpec(memory_space=pltpu.VMEM),
         scratch_shapes=[

time: 46.5 us -> 41.9 us (0.901)
  Pallas kernels: 44.7 us -> 40.8 us
  local copies, waits for them, and re-layouts: 1.65 us -> 0.66 us
    pallas_call x1, Pallas kernels: 44.7 us -> 40.8 us  [local(): pl.pallas_call(functools.partial(kernel, stages), out_shape=pltpu.VMEM(rh...]
    unnamed x1, local copies, waits for them, and re-layouts: 1.65 us -> 0.66 us
where the time goes in v3:
time: 41.9 us; the launch traced here: 41.5 us
  Pallas kernels  40.8 us (97%)
  local copies, waits for them, and re-layouts  0.66 us (2%)
    pallas_call x1, Pallas kernels, local(): pl.pallas_call(functools.partial(kernel, stages), out_shape=pltpu.VMEM(rh...  40.8 us

profile of v3, /device:TPU:2, one launch (start us, length us, event | category | flops | bytes accessed | tf_op | source)
XLA Modules:
  0.0 41.5 jit_solution(9345252832232005467)
XLA Ops:
  0.0 40.8 %window_solve.1 = bf16[64,2,512]{2,1,0:T(2,128)(2,1)S(1)} custom-call(bf16[1024,3072]{1,0:T(8,128)(2,1)} %solved.1, bf16[2,512,3072]{2,1,0:T(8,128)(2,1)} %panel.1, bf16[2,512,4096]{2,1,0:T(8,128)(2,1)} %inverse.1, bf16[512,4096]{1,0:T(8,128)(2,1)} %link.1, bf16[64,2,512]{2,1,0:T(2,128)(2,1)} %rhs.1), custom_call_target="tpu_custom_call" | custom-call | flops 6442450944 | bytes 25165824 | tf_op jit(solution)/shard_map/window_solve/pallas_call | solution.py:324
  40.8 0.7 %copy.7 = bf16[64,2,512]{2,1,0:T(2,128)(2,1)} copy(bf16[64,2,512]{2,1,0:T(2,128)(2,1)S(1)} %window_solve.1) | data formatting | bytes 262144

commit v4 on v3

--- a/solution.py
+++ b/solution.py
@@ -25,7 +25,7 @@
 def kernel(
     stages, solved, panel, inverse, link, rhs, out,
     sol_v, pan_v, inv_v, lnk_v, rhs_v,
-    core_out, core_in, col_out, col_in, x_out, x_in, keep, acc,
+    core_out, core_in, own, col_out, col_in, x_out, x_in, keep, acc,
     part, a_out, a_in, f_all, c_out, c_in,
     load_sem, core_sem, col_sem, x_sem, a_sem, f_sem, c_sem,
 ):
@@ -141,26 +141,30 @@
         if b == 0:
             for s in range(SLOTS):
                 arrive("sol", 1, h, s)
-        if (b, h) == (1, 0):
+        if (b, h) == (0, 1):
             load(load_link, "link")
             load(load_inv[1], "inverse", 1)
-        total = dot(sol_v[1, h], pan_v[b], NT)
+        own[...] = dot(sol_v[1, h], pan_v[b], NT)
+
+    def add_sibling(b, h):
+        arrive("core", b, h)
+        last = 7 * part_rows
+        if b == 0:
+            col_out[0, h, slot_rows(0, 7)] = (own[:last] + core_in[0, h, :last].astype(F32)).astype(BF16)
+            for s in range(SLOTS - 1):
+                start(col_copy(h, s), "col", h, s)
+        else:
+            sent = 6 * part_rows
+            col_out[1, h, slot_rows(0, 6)] = (own[:sent] + core_in[1, h, :sent].astype(F32)).astype(BF16)
+            keep[h] = own[sent:last] + core_in[1, h, sent:last].astype(F32)
         if (b, h) == (0, 0):
             clear()
             take_rhs()
-        arrive("core", b, h)
-        total = total + core_in[b, h].astype(F32)
-        last = 7 * part_rows
-        if b == 0:
-            col_out[0, h, slot_rows(0, 7)] = total[:last].astype(BF16)
-            for s in range(SLOTS - 1):
-                start(col_copy(h, s), "col", h, s)
-        else:
-            col_out[1, h, slot_rows(0, 6)] = total[: 6 * part_rows].astype(BF16)
-            for i in range(3):
-                start(z_copy(h, i), "z", h, i)
-            keep[h] = total[6 * part_rows : last]
-        acc[b, h] -= total[last:]
+        acc[b, h] -= own[last:] + core_in[b, h, last:].astype(F32)
+
+    def z_send(h):
+        for i in range(3):
+            start(z_copy(h, i), "z", h, i)
 
     def first_residual(h):
         for s in range(SLOTS - 1):
@@ -268,13 +272,13 @@
             at = pl.ds(pl.multiple_of(owner * local_rows, local_rows), local_rows)
             return dot(f_all[h, owner], lnk_v[:, at], NT)
 
-        for other in range(2):
-            base = lax.rem(x_lo + other, 2) * 4
-            for i in range(4):
-                @pl.when(base + i != row)
-                def _():
-                    f_wait(h, base + i)
-            res = res - sum(term(base + i) for i in range(4))
+        y = lax.rem(row, 4)
+        for other, steps in ((0, (0, 1, 3, 2)), (1, (0, 1)), (1, (3, 2))):
+            owners = [lax.rem(x_lo + other, 2) * 4 + lax.rem(y + step, 4) for step in steps]
+            for owner, step in zip(owners, steps):
+                if other or step:
+                    f_wait(h, owner)
+            res = res - sum(term(owner) for owner in owners)
         solve_send(1, h, res.astype(BF16), c_out, c_in, c_sem)
 
     def finish(h):
@@ -295,12 +299,14 @@
 
     program = (
         lambda: sibling_part(0, 0), lambda: own_part(0, 0),
-        lambda: sibling_part(0, 1), lambda: own_part(0, 1),
-        lambda: sibling_part(1, 0), lambda: own_part(1, 0),
+        lambda: sibling_part(0, 1), lambda: add_sibling(0, 0), lambda: own_part(0, 1),
+        lambda: sibling_part(1, 0), lambda: add_sibling(0, 1), lambda: own_part(1, 0),
+        lambda: sibling_part(1, 1), lambda: add_sibling(1, 0),
+        lambda: own_part(1, 1),
         lambda: a_step(0),
-        lambda: sibling_part(1, 1),
+        lambda: z_send(0), lambda: add_sibling(1, 1),
         lambda: a_step(1),
-        lambda: own_part(1, 1),
+        lambda: z_send(1),
         lambda: first_send(0),
         lambda: second_sum_over_z(0),
         lambda: first_send(1),
@@ -334,6 +340,7 @@
             pltpu.VMEM(rhs.shape, BF16),
             pltpu.VMEM((2,) + column, BF16),
             pltpu.VMEM((2,) + column, BF16),
+            pltpu.VMEM((SLOTS * part_rows, local_rows), F32),
             pltpu.VMEM((2,) + column, BF16),
             pltpu.VMEM((2,) + column, BF16),
             pltpu.VMEM((HALVES,) + piece, BF16),

time: 41.9 us -> 43.6 us (1.041)
  Pallas kernels: 40.8 us -> 42.8 us
    pallas_call x1, Pallas kernels: 40.8 us -> 42.8 us  [local(): pl.pallas_call(functools.partial(kernel, stages), out_shape=pltpu.VMEM(rh...]
where the time goes in v4:
time: 43.6 us; the launch traced here: 43.5 us
  Pallas kernels  42.8 us (98%)
  local copies, waits for them, and re-layouts  0.66 us (2%)
    pallas_call x1, Pallas kernels, local(): pl.pallas_call(functools.partial(kernel, stages), out_shape=pltpu.VMEM(rh...  42.8 us

profile of v4, /device:TPU:2, one launch (start us, length us, event | category | flops | bytes accessed | tf_op | source)
XLA Modules:
  0.0 43.5 jit_solution(17473330164910025160)
XLA Ops:
  0.0 42.8 %window_solve.1 = bf16[64,2,512]{2,1,0:T(2,128)(2,1)S(1)} custom-call(bf16[1024,3072]{1,0:T(8,128)(2,1)} %solved.1, bf16[2,512,3072]{2,1,0:T(8,128)(2,1)} %panel.1, bf16[2,512,4096]{2,1,0:T(8,128)(2,1)} %inverse.1, bf16[512,4096]{1,0:T(8,128)(2,1)} %link.1, bf16[64,2,512]{2,1,0:T(2,128)(2,1)} %rhs.1), custom_call_target="tpu_custom_call" | custom-call | flops 6442450944 | bytes 25165824 | tf_op jit(solution)/shard_map/window_solve/pallas_call | solution.py:330
  42.8 0.7 %copy.7 = bf16[64,2,512]{2,1,0:T(2,128)(2,1)} copy(bf16[64,2,512]{2,1,0:T(2,128)(2,1)S(1)} %window_solve.1) | data formatting | bytes 262144

commit v5 on v4

--- a/solution.py
+++ b/solution.py
@@ -13,8 +13,9 @@
 NT = (((1,), (1,)), ((), ()))
 NN = (((1,), (0,)), ((), ()))
 ROWS = 8
+F_ORDER = ((1, 2), (1, 1), (1, 3), (0, 2), (1, 0), (0, 1), (0, 3))
 SLOTS = 8
-Z_OFFSETS = (2, 1, 3, 0)
+Y_OFFSETS = Z_OFFSETS = (2, 1, 3, 0)
 HALVES = 2
 
 
@@ -32,7 +33,7 @@
     samples, local_rows = rhs.shape[0], rhs.shape[2]
     part_rows = samples // HALVES
     row, col = lax.axis_index("row"), lax.axis_index("col")
-    x_lo = row // 4
+    x_lo, y = row // 4, row % 4
     x_hi, z, core = col // 8, (col // 2) % 4, col % 2
     drains, arrivals = [], {}
 
@@ -189,21 +190,23 @@
         return remote(outgoing.at[h, j], incoming.at[h, row], sems.at[0, h, j], sems.at[1, h, row], (j, col))
 
     def solve_send(b, h, res, outgoing, incoming, sems):
-        def group(js):
-            for j in js:
+        def group(base):
+            for j in range(4 * base, 4 * base + 4):
                 product = dot(res, inv_v[b, :, j * local_rows : (j + 1) * local_rows], NN)
                 part[b, h, j] = product
                 outgoing[h, j] = product.astype(BF16)
-            for j in js:
+            for dy in Y_OFFSETS:
+                j = 4 * base + lax.rem(y + dy, 4)
+
                 @pl.when(row < j)
                 def _():
                     solve_copy(outgoing, incoming, sems, h, j).start()
 
-        group(range(ROWS - 1, 3, -1))
+        group(1)
 
         @pl.when(row < 4)
         def _():
-            group(range(3, -1, -1))
+            group(0)
 
         def drain():
             for j in range(1, ROWS):
@@ -240,9 +243,10 @@
                 c_in[:, i] = jnp.zeros_like(c_in[:, i])
 
     def f_copy(h, i):
+        dx, dy = F_ORDER[i]
         return remote(
             f_all.at[h, row], f_all.at[h, row], f_sem.at[0, h, i], f_sem.at[1, h, row],
-            (lax.rem(row + i, ROWS), col),
+            (lax.rem(x_lo + dx, 2) * 4 + lax.rem(y + dy, 4), col),
         )
 
     def f_wait(h, owner):
@@ -252,7 +256,7 @@
 
     def first_send(h):
         f_all[h, row] = solve_receive(0, h, a_in)
-        for i in (6, 5, 7, 4, 3, 2, 1):
+        for i in range(ROWS - 1):
             copy = f_copy(h, i)
             copy.start()
             drains.append(copy.wait_send)
@@ -272,7 +276,6 @@
             at = pl.ds(pl.multiple_of(owner * local_rows, local_rows), local_rows)
             return dot(f_all[h, owner], lnk_v[:, at], NT)
 
-        y = lax.rem(row, 4)
         for other, steps in ((0, (0, 1, 3, 2)), (1, (0, 1)), (1, (3, 2))):
             owners = [lax.rem(x_lo + other, 2) * 4 + lax.rem(y + step, 4) for step in steps]
             for owner, step in zip(owners, steps):

time: 43.6 us -> 42.9 us (0.984)
  Pallas kernels: 42.8 us -> 42.1 us
    pallas_call x1, Pallas kernels: 42.8 us -> 42.1 us  [local(): pl.pallas_call(functools.partial(kernel, stages), out_shape=pltpu.VMEM(rh...]
where the time goes in v5:
time: 42.9 us; the launch traced here: 42.8 us
  Pallas kernels  42.1 us (98%)
  local copies, waits for them, and re-layouts  0.66 us (2%)
    pallas_call x1, Pallas kernels, local(): pl.pallas_call(functools.partial(kernel, stages), out_shape=pltpu.VMEM(rh...  42.1 us

profile of v5, /device:TPU:2, one launch (start us, length us, event | category | flops | bytes accessed | tf_op | source)
XLA Modules:
  0.0 42.8 jit_solution(11254733801716857800)
XLA Ops:
  0.0 42.1 %window_solve.1 = bf16[64,2,512]{2,1,0:T(2,128)(2,1)S(1)} custom-call(bf16[1024,3072]{1,0:T(8,128)(2,1)} %solved.1, bf16[2,512,3072]{2,1,0:T(8,128)(2,1)} %panel.1, bf16[2,512,4096]{2,1,0:T(8,128)(2,1)} %inverse.1, bf16[512,4096]{1,0:T(8,128)(2,1)} %link.1, bf16[64,2,512]{2,1,0:T(2,128)(2,1)} %rhs.1), custom_call_target="tpu_custom_call" | custom-call | flops 6442450944 | bytes 25165824 | tf_op jit(solution)/shard_map/window_solve/pallas_call | solution.py:333
  42.1 0.7 %copy.7 = bf16[64,2,512]{2,1,0:T(2,128)(2,1)} copy(bf16[64,2,512]{2,1,0:T(2,128)(2,1)S(1)} %window_solve.1) | data formatting | bytes 262144

commit v6 on v5

--- a/solution.py
+++ b/solution.py
@@ -269,8 +269,7 @@
 
     def carry(h):
         arrivals.pop(("f", h))
-        arrive("x", h)
-        res = acc[1, h] - x_in[h].astype(F32)
+        res = acc[1, h]
 
         def term(owner):
             at = pl.ds(pl.multiple_of(owner * local_rows, local_rows), local_rows)
@@ -282,6 +281,8 @@
                 if other or step:
                     f_wait(h, owner)
             res = res - sum(term(owner) for owner in owners)
+        arrive("x", h)
+        res = res - x_in[h].astype(F32)
         solve_send(1, h, res.astype(BF16), c_out, c_in, c_sem)
 
     def finish(h):
@@ -305,15 +306,14 @@
         lambda: sibling_part(0, 1), lambda: add_sibling(0, 0), lambda: own_part(0, 1),
         lambda: sibling_part(1, 0), lambda: add_sibling(0, 1), lambda: own_part(1, 0),
         lambda: sibling_part(1, 1), lambda: add_sibling(1, 0),
-        lambda: own_part(1, 1),
+        lambda: z_send(0), lambda: own_part(1, 1),
         lambda: a_step(0),
-        lambda: z_send(0), lambda: add_sibling(1, 1),
+        lambda: add_sibling(1, 1), lambda: z_send(1),
         lambda: a_step(1),
-        lambda: z_send(1),
+        lambda: second_sum_over_z(0),
         lambda: first_send(0),
-        lambda: second_sum_over_z(0),
+        lambda: second_sum_over_z(1),
         lambda: first_send(1),
-        lambda: second_sum_over_z(1),
         lambda: carry_step(0), lambda: carry_step(1),
         lambda: finish(0), lambda: finish(1),
     )

time: 42.9 us -> 39.5 us (0.921)
  Pallas kernels: 42.1 us -> 38.4 us
    pallas_call x1, Pallas kernels: 42.1 us -> 38.4 us  [local(): pl.pallas_call(functools.partial(kernel, stages), out_shape=pltpu.VMEM(rh...]
where the time goes in v6:
time: 39.5 us; the launch traced here: 39.1 us
  Pallas kernels  38.4 us (97%)
  local copies, waits for them, and re-layouts  0.66 us (2%)
    pallas_call x1, Pallas kernels, local(): pl.pallas_call(functools.partial(kernel, stages), out_shape=pltpu.VMEM(rh...  38.4 us

profile of v6, /device:TPU:2, one launch (start us, length us, event | category | flops | bytes accessed | tf_op | source)
XLA Modules:
  0.0 39.1 jit_solution(2257088936402388682)
XLA Ops:
  0.0 38.4 %window_solve.1 = bf16[64,2,512]{2,1,0:T(2,128)(2,1)S(1)} custom-call(bf16[1024,3072]{1,0:T(8,128)(2,1)} %solved.1, bf16[2,512,3072]{2,1,0:T(8,128)(2,1)} %panel.1, bf16[2,512,4096]{2,1,0:T(8,128)(2,1)} %inverse.1, bf16[512,4096]{1,0:T(8,128)(2,1)} %link.1, bf16[64,2,512]{2,1,0:T(2,128)(2,1)} %rhs.1), custom_call_target="tpu_custom_call" | custom-call | flops 6442450944 | bytes 25165824 | tf_op jit(solution)/shard_map/window_solve/pallas_call | solution.py:333
  38.4 0.7 %copy.7 = bf16[64,2,512]{2,1,0:T(2,128)(2,1)} copy(bf16[64,2,512]{2,1,0:T(2,128)(2,1)S(1)} %window_solve.1) | data formatting | bytes 262144

commit v7 on v6

--- a/solution.py
+++ b/solution.py
@@ -13,7 +13,7 @@
 NT = (((1,), (1,)), ((), ()))
 NN = (((1,), (0,)), ((), ()))
 ROWS = 8
-F_ORDER = ((1, 2), (1, 1), (1, 3), (0, 2), (1, 0), (0, 1), (0, 3))
+F_ORDER = ((1, 2), (0, 2), (1, 1), (1, 3), (0, 1), (0, 3), (1, 0))
 SLOTS = 8
 Y_OFFSETS = Z_OFFSETS = (2, 1, 3, 0)
 HALVES = 2

time: 39.5 us -> 39.5 us (level)
  no operation moved by 1% of the time
where the time goes in v7:
time: 39.5 us; the launch traced here: 39.1 us
  Pallas kernels  38.4 us (97%)
  local copies, waits for them, and re-layouts  0.66 us (2%)
    pallas_call x1, Pallas kernels, local(): pl.pallas_call(functools.partial(kernel, stages), out_shape=pltpu.VMEM(rh...  38.4 us

profile of v7, /device:TPU:2, one launch (start us, length us, event | category | flops | bytes accessed | tf_op | source)
XLA Modules:
  0.0 39.1 jit_solution(16445992209965878057)
XLA Ops:
  0.0 38.4 %window_solve.1 = bf16[64,2,512]{2,1,0:T(2,128)(2,1)S(1)} custom-call(bf16[1024,3072]{1,0:T(8,128)(2,1)} %solved.1, bf16[2,512,3072]{2,1,0:T(8,128)(2,1)} %panel.1, bf16[2,512,4096]{2,1,0:T(8,128)(2,1)} %inverse.1, bf16[512,4096]{1,0:T(8,128)(2,1)} %link.1, bf16[64,2,512]{2,1,0:T(2,128)(2,1)} %rhs.1), custom_call_target="tpu_custom_call" | custom-call | flops 6442450944 | bytes 25165824 | tf_op jit(solution)/shard_map/window_solve/pallas_call | solution.py:333
  38.4 0.7 %copy.7 = bf16[64,2,512]{2,1,0:T(2,128)(2,1)} copy(bf16[64,2,512]{2,1,0:T(2,128)(2,1)S(1)} %window_solve.1) | data formatting | bytes 262144
